TPU v7x, 32 devices: a whole 2x2x4 slice. The times are simulated.
32 devices in a mesh: tm: 4 (over x, core), range: 8 (over z, y).
Axes of the slice: x: 2, y: 2, z: 4, core: 2. Of those that a mesh axis runs over, the one named last changes fastest.
Arguments:
- slc_stack: bfloat16 [16, 2, 8192, 128], P('tm', None, 'range'), as said below
- pair_list: int32 [24, 2], P('tm'), may hold values from 0 to 15, as said below
Outputs:
- coherence_field: bfloat16 [24, 2, 8192, 128], P('tm', None, 'range')
Inputs may be any that keep to these rules, and one draw needn't show every extreme that they name: `pair_list`: rows g * 6 to (g + 1) * 6 - 1 hold pairs whose reference (column 0) is one of the acquisitions g * 4 to (g + 1) * 4 - 1; the secondary (column 1) comes 1 to 3 acquisitions after the reference; no pair repeats. `slc_stack`: acquisitions of one scene with acquisition-dependent phase and noise.
All inputs are finite; a program needn't handle non-finite values.
Results may differ from a plain program's by a relative error of at most 0.001.
Values may be sent and summed in bfloat16 or wider, within the bound.
A program may use at most 64 MiB of HBM per device.

v0:
```python
import jax
import jax.numpy as jnp
from jax import lax
from jax.sharding import PartitionSpec as P

LAG_MAX = 3
LOOK_AZ = 5
LOOK_RG = 20


EPSILON = 1e-06


def passed_along(shard, axis, by):
    size = lax.axis_size(axis)
    pairs = [(i, i + by) for i in range(size) if 0 <= i + by < size]
    return lax.ppermute(shard, axis, pairs)


def box_both(values):
    lead_dims = values.shape[:-2]
    ext_cols = values.shape[-2]
    line_count = values.shape[-1]
    col_count = ext_cols - (LOOK_RG - 1)
    block_count = col_count // 128
    flattened = values.reshape((-1, ext_cols, line_count))
    padded = jnp.pad(flattened, ((0, 0), (0, col_count + 128 - ext_cols), (0, 0)))
    head_block = padded[:, 0:col_count].reshape((-1, block_count, 128, line_count))
    tail_block = padded[:, 128 : col_count + 128].reshape((-1, block_count, 128, line_count))
    row_index = lax.broadcasted_iota(jnp.int32, (128, 128), 0)
    col_index = lax.broadcasted_iota(jnp.int32, (128, 128), 1)
    offset_near = row_index - col_index
    offset_far = row_index + 128 - col_index
    band_near = ((offset_near >= 0) & (offset_near < LOOK_RG)).astype(jnp.float32)
    band_far = ((offset_far >= 0) & (offset_far < LOOK_RG)).astype(jnp.float32)
    running = jnp.einsum("kbil,io->kbol", head_block, band_near, precision=lax.Precision.HIGHEST)
    running = running + jnp.einsum(
        "kbil,io->kbol", tail_block, band_far, precision=lax.Precision.HIGHEST
    )
    running = running.reshape((-1, col_count, line_count))
    half_box = LOOK_AZ // 2
    padded = jnp.pad(running, ((0, 0), (0, 0), (half_box, LOOK_AZ - 1 - half_box)))
    summed = padded[:, :, 0:line_count]
    for j in range(1, LOOK_AZ):
        summed = summed + padded[:, :, j : j + line_count]
    return summed.reshape(lead_dims + (col_count, line_count))


def local(slc_stack, pair_list):
    acq_dev = slc_stack.shape[0]
    rim_width = LOOK_RG - 1
    n_range = lax.axis_size("range")
    first_acq = lax.axis_index("tm") * acq_dev
    at_end = lax.axis_index("range") == n_range - 1
    own_rim = passed_along(slc_stack[:, :, 0:rim_width, :], "range", -1)
    own_ext = jnp.concatenate([slc_stack, own_rim], axis=2)
    outgoing = slc_stack[0:LAG_MAX]
    received = passed_along(outgoing, "tm", -1)
    corner = passed_along(slc_stack[0:LAG_MAX, :, 0:rim_width, :], ("tm", "range"), -(n_range + 1))
    corner = jnp.where(at_end, jnp.zeros_like(corner), corner)
    next_ext = jnp.concatenate([received, corner], axis=2)
    stack_all = jnp.concatenate([own_ext, next_ext], axis=0)
    real_part = stack_all[:, 0].astype(jnp.float32)
    imag_part = stack_all[:, 1].astype(jnp.float32)
    powers_boxed = box_both(real_part * real_part + imag_part * imag_part)
    ref_index = pair_list[:, 0] - first_acq
    sec_index = pair_list[:, 1] - first_acq
    ref_data = jnp.take(stack_all, ref_index, axis=0).astype(jnp.float32)
    sec_data = jnp.take(stack_all, sec_index, axis=0).astype(jnp.float32)
    products = jnp.stack(
        [
            ref_data[:, 0] * sec_data[:, 0] + ref_data[:, 1] * sec_data[:, 1],
            ref_data[:, 1] * sec_data[:, 0] - ref_data[:, 0] * sec_data[:, 1],
        ],
        axis=1,
    )
    summed = box_both(products)
    inverse_norm = lax.rsqrt(
        jnp.take(powers_boxed, ref_index, axis=0) * jnp.take(powers_boxed, sec_index, axis=0)
        + EPSILON
    )
    return (summed * inverse_norm[:, None]).astype(jnp.bfloat16)


def solution(mesh):
    in_specs = (P("tm", None, "range", None), P("tm", None))
    out_specs = P("tm", None, "range", None)
    return jax.shard_map(local, mesh=mesh, in_specs=in_specs, out_specs=out_specs, check_vma=False)
```

profile of v0, /device:TPU:17, one launch (start us, length us, event | category | flops | bytes accessed | tf_op | source)
XLA Modules:
  0.0 98.5 jit_solution(7339834196676513621)
XLA Ops:
  0.0 0.0 copy-start.3
  0.0 2.8 %slice.78 = bf16[3,2,1024,128]{3,2,1,0:T(8,128)(2,1)} slice(bf16[4,2,1024,128]{3,2,1,0:T(8,128)(2,1)} %param.6), slice={[0:3], [0:2], [0:1024], [0:128]} | slice | bytes 3145728 | tf_op jit(solution)/shard_map/slice | solution.py:57
  2.8 2.6 %collective-permute-start.1 = (bf16[3,2,1024,128]{3,2,1,0:T(8,128)(2,1)}, bf16[3,2,1024,128]{3,2,1,0:T(8,128)(2,1)}, u32[]{:S(2)}, u32[]{:S(2)}) collective-permute-start(bf16[3,2,1024,128]{3,2,1,0:T(8,128)(2,1)} %slice.78), channel_id=1, source_target_pairs={{8,0},{16,8},{24,16},{9,1},{17,9},{25,17},{10,2},{18,10},{26,18},{... | collective-permute-start | bytes 4718600 | tf_op jit(solution)/shard_map/ppermute | solution.py:17
  5.4 0.8 slice.79
  6.2 2.3 %collective-permute-start.2 = (bf16[3,2,19,128]{3,2,1,0:T(8,128)(2,1)S(1)}, bf16[3,2,19,128]{3,2,1,0:T(8,128)(2,1)S(1)}, u32[]{:S(2)}, u32[]{:S(2)}) collective-permute-start(bf16[3,2,19,128]{3,2,1,0:T(8,128)(2,1)S(1)} %slice.79), channel_id=1, source_target_pairs={{9,0},{10,1},{11,2},{12,3},{13,4},{14,5},{15,6},{16,7},{17,8},{18,... | collective-permute-start | bytes 87560 | tf_op jit(solution)/shard_map/ppermute | solution.py:17
  8.5 0.8 slice.77
  9.3 2.6 %collective-permute-start = (bf16[4,2,19,128]{3,2,1,0:T(8,128)(2,1)S(1)}, bf16[4,2,19,128]{3,2,1,0:T(8,128)(2,1)S(1)}, u32[]{:S(2)}, u32[]{:S(2)}) collective-permute-start(bf16[4,2,19,128]{3,2,1,0:T(8,128)(2,1)S(1)} %slice.77), channel_id=1, source_target_pairs={{1,0},{2,1},{3,2},{4,3},{5,4},{6,5},{7,6},{9,8},{10,9},{11,10},{12... | collective-permute-start | bytes 116744 | tf_op jit(solution)/shard_map/ppermute | solution.py:17
  11.9 0.8 compare_and_fusion.1
  12.7 13.4 %collective-permute-done.2 = bf16[3,2,19,128]{3,2,1,0:T(8,128)(2,1)S(1)} collective-permute-done((bf16[3,2,19,128]{3,2,1,0:T(8,128)(2,1)S(1)}, bf16[3,2,19,128]{3,2,1,0:T(8,128)(2,1)S(1)}, u32[]{:S(2)}, u32[]{:S(2)}) %collective-permute-start.2) | collective-permute-done | bytes 29216 | tf_op jit(solution)/shard_map/ppermute | solution.py:17
  26.1 0.0 collective-permute-done
  26.1 0.0 collective-permute-done.1
  26.2 0.0 copy-done.3
  26.2 1.5 %maximum_maximum_fusion = bf16[7,2,1043,128]{3,2,1,0:T(8,128)(2,1)S(1)} fusion(bf16[3,2,19,128]{3,2,1,0:T(8,128)(2,1)S(1)} %broadcast_select_fusion, bf16[3,2,1024,128]{3,2,1,0:T(8,128)(2,1)} %collective-permute-done.1, bf16[4,2,19,128]{3,2,1,0:T(8,128)(2,1)S(1)} %collective-permute-done, bf16[4,2,1024,128]{3,2,1,0:T(8,128)(2,1)S(1)} %copy-done.3), kind=kLoop, calls=%fused_computation.20 | loop fusion | flops 14952448 | bytes 7476224 | tf_op jit(solution)/shard_map/concatenate | solution.py:62
  27.7 0.0 copy-start
  27.7 1.8 %copy-done = bf16[7,2,1043,128]{3,2,1,0:T(8,128)(2,1)} copy-done((bf16[7,2,1043,128]{3,2,1,0:T(8,128)(2,1)}, bf16[7,2,1043,128]{3,2,1,0:T(8,128)(2,1)S(1)}, u32[]{:S(2)}) %copy-start) | copy-done | bytes 3738136
  29.5 2.5 %add_bitcast_fusion = f32[7,1043,128]{2,1,0:T(8,128)} fusion(bf16[7,2,1043,128]{3,2,1,0:T(8,128)(2,1)S(1)} %maximum_maximum_fusion), kind=kLoop, calls=%fused_computation.21 | loop fusion | flops 4672640 | bytes 7476224 | tf_op jit(solution)/shard_map/add | solution.py:65
  32.0 3.2 %gather_fusion.1 = bf16[6,2,1043,128]{3,2,1,0:T(8,128)(2,1)S(1)} fusion(bf16[7,2,1043,128]{3,2,1,0:T(8,128)(2,1)} %copy-done, s32[1024]{0:T(1024)S(1)} %pad_clamp_fusion), kind=kCustom, calls=%fused_computation.2.clone | custom fusion | bytes 6408216 | tf_op jit(solution)/shard_map/jit(_take)/gather | solution.py:69
  35.2 4.9 %gather_fusion = bf16[6,2,1043,128]{3,2,1,0:T(8,128)(2,1)} fusion(bf16[7,2,1043,128]{3,2,1,0:T(8,128)(2,1)} %copy-done, s32[1024]{0:T(1024)S(1)} %pad_clamp_fusion.1), kind=kCustom, calls=%fused_computation.clone | custom fusion | bytes 6408216 | tf_op jit(solution)/shard_map/jit(_take)/gather | solution.py:68
  40.1 3.7 %pad_slice_fusion.9 = (f32[7,1024,128]{2,1,0:T(8,128)S(1)}, f32[7,1024,128]{2,1,0:T(8,128)S(1)}) fusion(f32[7,1043,128]{2,1,0:T(8,128)} %add_bitcast_fusion), kind=kLoop, calls=%fused_computation.19 | loop fusion | bytes 14766080 | tf_op jit(solution)/shard_map/slice | solution.py:29
  43.9 2.1 %fusion.18 = f32[128,7,8,128]{3,0,2,1:T(8,128)S(1)} fusion(f32[7,8,128,128]{3,2,1,0:T(8,128)S(1)} %bitcast.43), kind=kOutput, calls=%fused_computation.45 | convolution fusion | flops 1409351680 | bytes 7340032 | tf_op jit(solution)/shard_map/kbil,io->kbol/dot_general | solution.py:36
  46.0 2.5 %convolution_add_fusion.1 = f32[128,7,8,128]{3,0,2,1:T(8,128)S(1)} fusion(f32[128,7,8,128]{3,0,2,1:T(8,128)S(1)} %fusion.18, f32[7,8,128,128]{3,2,1,0:T(8,128)S(1)} %bitcast.45, s32[128]{0:T(128)S(1)} %iota_add_fusion), kind=kOutput, calls=%fused_computation.34 | convolution fusion | flops 1410269184 | bytes 11010560 | tf_op jit(solution)/shard_map/kbil,io->kbol/dot_general | solution.py:37
  48.5 5.6 %fusion.7 = f32[7,1024,128]{2,1,0:T(8,128)} fusion(f32[7,1024,128]{2,1,0:T(8,128)S(1)} %bitcast.44), kind=kLoop, calls=%fused_computation.25 | loop fusion | flops 3670016 | bytes 7340032 | tf_op jit(solution)/shard_map/add | solution.py:45
  54.2 4.4 %gather_fusion.3 = f32[6,1024,128]{2,1,0:T(8,128)} fusion(f32[7,1024,128]{2,1,0:T(8,128)} %fusion.7, s32[1024]{0:T(1024)S(1)} %pad_clamp_fusion), kind=kCustom, calls=%fused_computation.3.clone | custom fusion | bytes 6291480 | tf_op jit(solution)/shard_map/jit(_take)/gather | solution.py:79
  58.6 4.4 %gather_fusion.2 = f32[6,1024,128]{2,1,0:T(8,128)} fusion(f32[7,1024,128]{2,1,0:T(8,128)} %fusion.7, s32[1024]{0:T(1024)S(1)} %pad_clamp_fusion.1), kind=kCustom, calls=%fused_computation.1.clone | custom fusion | bytes 6291480 | tf_op jit(solution)/shard_map/jit(_take)/gather | solution.py:79
  63.0 2.8 %select_convert_fusion = (f32[6,2,1043,128]{3,2,1,0:T(8,128)S(1)}, f32[6,2,1043,128]{3,2,1,0:T(8,128)S(1)}) fusion(bf16[6,2,1043,128]{3,2,1,0:T(8,128)(2,1)S(1)} %gather_fusion.1, pred[6]{0:T(512)(128)(4,1)S(1)} %get-tuple-element.17, bf16[6,2,1043,128]{3,2,1,0:T(8,128)(2,1)} %gather_fusion, pred[6]{0:T(512)(128)(4,1)S(1)} %get-tuple-element.6), kind=kLoop, calls=%fused_computation.26 | loop fusion | flops 6408192 | bytes 19224588 | tf_op jit(solution)/shard_map/convert_element_type | solution.py:69
  65.9 3.4 %multiply_add_fusion = (f32[6,1,1043,128]{3,2,1,0:T(8,128)}, f32[6,1,1043,128]{3,2,1,0:T(8,128)}) fusion(f32[6,2,1043,128]{3,2,1,0:T(8,128)S(1)} %get-tuple-element.19, f32[6,2,1043,128]{3,2,1,0:T(8,128)S(1)} %get-tuple-element.20), kind=kLoop, calls=%fused_computation.29 | loop fusion | flops 4806144 | bytes 19224576 | tf_op jit(solution)/shard_map/add | solution.py:72
  69.2 3.5 %pad_maximum_fusion = f32[6,2,1043,128]{3,2,1,0:T(8,128)S(1)} fusion(f32[6,1,1043,128]{3,2,1,0:T(8,128)} %get-tuple-element.12, f32[6,1,1043,128]{3,2,1,0:T(8,128)} %get-tuple-element.11), kind=kLoop, calls=%fused_computation.13 | loop fusion | flops 1602048 | bytes 12816384 | tf_op jit(solution)/shard_map/stack | solution.py:70
  72.7 6.0 %pad_slice_fusion.8 = (f32[12,1024,128]{2,1,0:T(8,128)}, f32[12,1024,128]{2,1,0:T(8,128)}) fusion(f32[12,1043,128]{2,1,0:T(8,128)S(1)} %bitcast.36), kind=kLoop, calls=%fused_computation.12 | loop fusion | bytes 25313280 | tf_op jit(solution)/shard_map/slice | solution.py:29
  78.7 0.0 slice-start
  78.7 0.0 slice-start.1
  78.7 5.7 %fusion.20 = f32[128,12,8,128]{3,0,2,1:T(8,128)S(1)} fusion(f32[12,8,128,128]{3,2,1,0:T(8,128)} %bitcast.38), kind=kOutput, calls=%fused_computation.46 | convolution fusion | flops 2415984640 | bytes 12582912 | tf_op jit(solution)/shard_map/kbil,io->kbol/dot_general | solution.py:36
  84.4 0.0 slice-done
  84.4 0.0 slice-done.1
  84.4 4.5 %convolution_add_fusion = f32[128,12,8,128]{3,0,2,1:T(8,128)S(1)} fusion(f32[128,12,8,128]{3,0,2,1:T(8,128)S(1)} %fusion.20, f32[12,8,128,128]{3,2,1,0:T(8,128)S(1)} %bitcast.42, s32[128]{0:T(128)S(1)} %iota_add_fusion), kind=kOutput, calls=%fused_computation.33 | convolution fusion | flops 2417557504 | bytes 18874880 | tf_op jit(solution)/shard_map/kbil,io->kbol/dot_general | solution.py:37
  89.0 0.0 copy-start.1
  89.0 0.0 copy-start.2
  89.0 6.6 %fusion.3 = f32[12,1024,128]{2,1,0:T(8,128)S(1)} fusion(f32[12,1024,128]{2,1,0:T(8,128)S(1)} %bitcast.39), kind=kLoop, calls=%fused_computation.17 | loop fusion | flops 6291456 | bytes 12582912 | tf_op jit(solution)/shard_map/add | solution.py:45
  95.6 0.0 copy-done.1
  95.6 0.0 copy-done.2
  95.7 0.6 fusion.9
  96.2 2.2 %multiply_convert_fusion = bf16[6,2,1024,128]{3,2,1,0:T(8,128)(2,1)} fusion(f32[6,2,1024,128]{3,2,1,0:T(8,128)S(1)} %bitcast.37, f32[6,1024,128]{2,1,0:T(8,128)S(1)} %fusion.9), kind=kLoop, calls=%fused_computation.18 | loop fusion | flops 3145728 | bytes 12582912 | tf_op jit(solution)/shard_map/convert_element_type | solution.py:82
  (5 shorter events, 0.0 us)
Async XLA Ops:
  0.0 26.2 %copy-start.3 = (bf16[4,2,1024,128]{3,2,1,0:T(8,128)(2,1)S(1)}, bf16[4,2,1024,128]{3,2,1,0:T(8,128)(2,1)}, u32[]{:S(2)}) copy-start(bf16[4,2,1024,128]{3,2,1,0:T(8,128)(2,1)} %param.6) | copy-start | bytes 6291460
  2.8 23.3 %collective-permute-start.1 = (bf16[3,2,1024,128]{3,2,1,0:T(8,128)(2,1)}, bf16[3,2,1024,128]{3,2,1,0:T(8,128)(2,1)}, u32[]{:S(2)}, u32[]{:S(2)}) collective-permute-start(bf16[3,2,1024,128]{3,2,1,0:T(8,128)(2,1)} %slice.78), channel_id=1, source_target_pairs={{8,0},{16,8},{24,16},{9,1},{17,9},{25,17},{10,2},{18,10},{26,18},{... | collective-permute-start | bytes 4718600 | tf_op jit(solution)/shard_map/ppermute | solution.py:17
  6.2 20.0 %collective-permute-start.2 = (bf16[3,2,19,128]{3,2,1,0:T(8,128)(2,1)S(1)}, bf16[3,2,19,128]{3,2,1,0:T(8,128)(2,1)S(1)}, u32[]{:S(2)}, u32[]{:S(2)}) collective-permute-start(bf16[3,2,19,128]{3,2,1,0:T(8,128)(2,1)S(1)} %slice.79), channel_id=1, source_target_pairs={{9,0},{10,1},{11,2},{12,3},{13,4},{14,5},{15,6},{16,7},{17,8},{18,... | collective-permute-start | bytes 87560 | tf_op jit(solution)/shard_map/ppermute | solution.py:17
  9.3 16.9 %collective-permute-start = (bf16[4,2,19,128]{3,2,1,0:T(8,128)(2,1)S(1)}, bf16[4,2,19,128]{3,2,1,0:T(8,128)(2,1)S(1)}, u32[]{:S(2)}, u32[]{:S(2)}) collective-permute-start(bf16[4,2,19,128]{3,2,1,0:T(8,128)(2,1)S(1)} %slice.77), channel_id=1, source_target_pairs={{1,0},{2,1},{3,2},{4,3},{5,4},{6,5},{7,6},{9,8},{10,9},{11,10},{12... | collective-permute-start | bytes 116744 | tf_op jit(solution)/shard_map/ppermute | solution.py:17
  27.7 1.8 %copy-start = (bf16[7,2,1043,128]{3,2,1,0:T(8,128)(2,1)}, bf16[7,2,1043,128]{3,2,1,0:T(8,128)(2,1)S(1)}, u32[]{:S(2)}) copy-start(bf16[7,2,1043,128]{3,2,1,0:T(8,128)(2,1)S(1)} %maximum_maximum_fusion) | copy-start | bytes 11214340
  78.7 5.7 %slice-start = ((s8[6291456]{0:T(1024)(128)(4,1)}), s8[4194304]{0:T(1024)(128)(4,1)S(1)}, s32[]{:S(2)}) async-start(s8[6291456]{0:T(1024)(128)(4,1)} %bitcast.40), calls=%async_computation | async-start | bytes 8388608
  78.7 5.7 %slice-start.1 = ((s8[6291456]{0:T(1024)(128)(4,1)}), s8[2097152]{0:T(1024)(128)(4,1)S(1)}, s32[]{:S(2)}) async-start(s8[6291456]{0:T(1024)(128)(4,1)} %bitcast.40), calls=%async_computation.1 | async-start | bytes 4194304
  89.0 6.7 %copy-start.1 = (f32[6,1024,128]{2,1,0:T(8,128)S(1)}, f32[6,1024,128]{2,1,0:T(8,128)}, u32[]{:S(2)}) copy-start(f32[6,1024,128]{2,1,0:T(8,128)} %gather_fusion.3) | copy-start | bytes 9437188
  89.0 6.7 %copy-start.2 = (f32[6,1024,128]{2,1,0:T(8,128)S(1)}, f32[6,1024,128]{2,1,0:T(8,128)}, u32[]{:S(2)}) copy-start(f32[6,1024,128]{2,1,0:T(8,128)} %gather_fusion.2) | copy-start | bytes 9437188
where the time goes:
time: 99.8 us; the launch traced here: 98.5 us
  local copies, waits for them, and re-layouts  32.9 us (33%)
  other arithmetic  29.5 us (30%)
  matrix products  14.9 us (15%)
  waiting for transfers between devices  13.4 us (13%)
  starting transfers between devices  7.5 us (8%)
    ppermute x3, waiting for transfers between devices, passed_along(): return lax.ppermute(shard, axis, pairs)  13.4 us
    add x2, other arithmetic, box_both(): summed = summed + padded[:, :, j:j + line_count]  12.3 us
    slice x2, local copies, waits for them, and re-layouts, box_both(): padded[:, 128:col_count + 128].reshape((-1, block_count, 128, line_count))  9.71 us
    dot_general x2, matrix products, box_both(): jnp.einsum('kbil,io->kbol', head_block, band_near, precision=lax.Precisio...  7.83 us
    ppermute x3, starting transfers between devices, passed_along(): return lax.ppermute(shard, axis, pairs)  7.5 us
    dot_general x2, matrix products, box_both(): jnp.einsum('kbil,io->kbol', tail_block, band_far, precision=lax.Precision...  7.05 us
    gather x1, local copies, waits for them, and re-layouts, local(): ref_data = jnp.take(stack_all, ref_index, axis=0).astype(jnp.float32)  4.9 us
    gather x1, local copies, waits for them, and re-layouts, local(): jnp.take(powers_boxed, sec_index, axis=0)  4.45 us
  transfers between devices with their start and end apart: 3, of which 1 were waited for; matrix products, arithmetic and copies ran while one was open for 2% of the time, Pallas kernels for 0%

commit v1 on v0

v1 whole, which is shorter than its diff:
```python
import functools

import jax
import jax.numpy as jnp
from jax import lax
from jax.experimental import pallas as pl
from jax.experimental.pallas import tpu as pltpu
from jax.sharding import PartitionSpec as P

LAG_MAX = 3
LOOK_AZ = 5
LOOK_RG = 20
RIM = 32
CHUNK = 128
EPSILON = 1e-06
MESH = pl.DeviceIdType.MESH


def kernel(
    n_tm,
    n_range,
    pair_ref,
    slc_ref,
    out_ref,
    own,
    recv,
    work,
    field,
    twos,
    fours,
    boxed,
    own_sem,
    send_sem,
    recv_sem,
    rim_send,
    rim_recv,
):
    tm = lax.axis_index("tm")
    rg = lax.axis_index("range")
    acq_dev, _, cols, lines = slc_ref.shape
    n_pairs = out_ref.shape[0]
    n_chunks = cols // CHUNK
    n_acq = acq_dev + LAG_MAX
    has_next = tm < n_tm - 1
    has_prev = tm > 0
    has_right = rg < n_range - 1
    has_left = rg > 0

    def own_copy(c):
        at = pl.ds(pl.multiple_of(c * CHUNK, CHUNK), CHUNK)
        return pltpu.make_async_copy(slc_ref.at[:, :, at, :], own.at[:, :, at, :], own_sem.at[c])

    def chunk_copy(c):
        at = pl.ds(pl.multiple_of(c * CHUNK, CHUNK), CHUNK)
        return pltpu.make_async_remote_copy(
            src_ref=slc_ref.at[pl.ds(0, LAG_MAX), :, at, :],
            dst_ref=recv.at[:, :, at, :],
            send_sem=send_sem.at[c],
            recv_sem=recv_sem.at[c],
            device_id=(tm - 1, rg),
            device_id_type=MESH,
        )

    rim_copy = pltpu.make_async_remote_copy(
        src_ref=slc_ref.at[:, :, pl.ds(0, RIM), :],
        dst_ref=own.at[:, :, pl.ds(cols, RIM), :],
        send_sem=rim_send.at[0],
        recv_sem=rim_recv.at[0],
        device_id=(tm, rg - 1),
        device_id_type=MESH,
    )
    corner_copy = pltpu.make_async_remote_copy(
        src_ref=slc_ref.at[pl.ds(0, LAG_MAX), :, pl.ds(0, RIM), :],
        dst_ref=recv.at[:, :, pl.ds(cols, RIM), :],
        send_sem=rim_send.at[1],
        recv_sem=rim_recv.at[1],
        device_id=(tm - 1, rg - 1),
        device_id_type=MESH,
    )

    barrier = pltpu.get_barrier_semaphore()

    @pl.when(has_next)
    def _():
        pl.semaphore_signal(barrier, inc=1, device_id=(tm + 1, rg), device_id_type=MESH)

    @pl.when(has_right)
    def _():
        pl.semaphore_signal(barrier, inc=1, device_id=(tm, rg + 1), device_id_type=MESH)

    @pl.when(has_next & has_right)
    def _():
        pl.semaphore_signal(barrier, inc=1, device_id=(tm + 1, rg + 1), device_id_type=MESH)

    @pl.loop(0, n_chunks)
    def _(i):
        own_copy(n_chunks - 1 - i).start()

    prev_count = jnp.where(has_prev, 1, 0)
    left_count = jnp.where(has_left, 1, 0)

    @pl.when(has_prev | has_left)
    def _():
        pl.semaphore_wait(barrier, prev_count + left_count + prev_count * left_count)

    @pl.when(has_left)
    def _():
        rim_copy.start()

    @pl.when(has_prev & has_left)
    def _():
        corner_copy.start()

    @pl.when(has_prev)
    def _():
        @pl.loop(0, n_chunks)
        def _(i):
            chunk_copy(n_chunks - 1 - i).start()

    @pl.when(jnp.logical_not(has_next))
    def _():
        recv[...] = jnp.zeros_like(recv)

    @pl.when(has_next & jnp.logical_not(has_right))
    def _():
        recv[:, :, cols:, :] = jnp.zeros((LAG_MAX, 2, RIM, lines), recv.dtype)

    @pl.when(jnp.logical_not(has_right))
    def _():
        own[:, :, cols:, :] = jnp.zeros((acq_dev, 2, RIM, lines), own.dtype)

    @pl.when(has_right)
    def _():
        rim_copy.wait_recv()

    @pl.when(has_next & has_right)
    def _():
        corner_copy.wait_recv()

    half = LOOK_AZ // 2
    from_line = lax.rem(lax.broadcasted_iota(jnp.int32, (2 * lines, lines), 0), lines)
    to_line = lax.broadcasted_iota(jnp.int32, (2 * lines, lines), 1)
    near = (from_line - to_line >= -half) & (from_line - to_line <= LOOK_AZ - 1 - half)
    band = jnp.where(near, 1.0, 0.0).astype(jnp.bfloat16)
    first_acq = tm * acq_dev

    def box(k, value):
        field[k] = value
        twos[k] = field[k, 0 : CHUNK + 24, :] + field[k, 1 : CHUNK + 25, :]
        fours[k] = twos[k, 0 : CHUNK + 16, :] + twos[k, 2 : CHUNK + 18, :]
        running = fours[k, 0:CHUNK, :]
        for j in range(4, LOOK_RG, 4):
            running = running + fours[k, j : j + CHUNK, :]
        high = running.astype(jnp.bfloat16)
        low = (running - high.astype(jnp.float32)).astype(jnp.bfloat16)
        return jnp.dot(
            jnp.concatenate([high, low], axis=1), band, preferred_element_type=jnp.float32
        )

    @pl.loop(0, n_chunks)
    def _(i):
        c = n_chunks - 1 - i
        own_copy(c).wait()

        @pl.when(has_next)
        def _():
            chunk_copy(c).wait_recv()

        start = pl.multiple_of(c * CHUNK, CHUNK)
        at = pl.ds(start, CHUNK)
        ext = pl.ds(start, CHUNK + RIM)
        for k in range(n_acq):
            source = own.at[k] if k < acq_dev else recv.at[k - acq_dev]
            real = source[0, ext, :].astype(jnp.float32)
            imag = source[1, ext, :].astype(jnp.float32)
            work[k, 0] = real
            work[k, 1] = imag
            boxed[k] = box(k % 2, real * real + imag * imag)
        for p in range(n_pairs):
            ref = jnp.clip(pair_ref[0, p] - first_acq, 0, n_acq - 1)
            sec = jnp.clip(pair_ref[1, p] - first_acq, 0, n_acq - 1)
            r0, r1 = work[ref, 0], work[ref, 1]
            s0, s1 = work[sec, 0], work[sec, 1]
            norm = lax.rsqrt(boxed[ref] * boxed[sec] + EPSILON)
            out_ref[p, 0, at, :] = (box(0, r0 * s0 + r1 * s1) * norm).astype(out_ref.dtype)
            out_ref[p, 1, at, :] = (box(1, r1 * s0 - r0 * s1) * norm).astype(out_ref.dtype)

    @pl.when(has_left)
    def _():
        rim_copy.wait_send()

    @pl.when(has_prev & has_left)
    def _():
        corner_copy.wait_send()

    @pl.when(has_prev)
    def _():
        @pl.loop(0, n_chunks)
        def _(i):
            chunk_copy(n_chunks - 1 - i).wait_send()


def local(slc_stack, pair_list):
    acq_dev, _, cols, lines = slc_stack.shape
    n_pairs = pair_list.shape[0]
    n_acq = acq_dev + LAG_MAX
    n_chunks = cols // CHUNK
    f32 = jnp.float32
    return pl.pallas_call(
        functools.partial(kernel, lax.axis_size("tm"), lax.axis_size("range")),
        out_shape=jax.ShapeDtypeStruct((n_pairs, 2, cols, lines), jnp.bfloat16),
        in_specs=[
            pl.BlockSpec(memory_space=pltpu.SMEM),
            pl.BlockSpec(memory_space=pltpu.HBM),
        ],
        out_specs=pl.BlockSpec(memory_space=pltpu.VMEM),
        scratch_shapes=[
            pltpu.VMEM((acq_dev, 2, cols + RIM, lines), jnp.bfloat16),
            pltpu.VMEM((LAG_MAX, 2, cols + RIM, lines), jnp.bfloat16),
            pltpu.VMEM((n_acq, 2, CHUNK + RIM, lines), f32),
            pltpu.VMEM((2, CHUNK + RIM, lines), f32),
            pltpu.VMEM((2, CHUNK + 24, lines), f32),
            pltpu.VMEM((2, CHUNK + 16, lines), f32),
            pltpu.VMEM((n_acq, CHUNK, lines), f32),
            pltpu.SemaphoreType.DMA((n_chunks,)),
            pltpu.SemaphoreType.DMA((n_chunks,)),
            pltpu.SemaphoreType.DMA((n_chunks,)),
            pltpu.SemaphoreType.DMA((2,)),
            pltpu.SemaphoreType.DMA((2,)),
        ],
        compiler_params=pltpu.CompilerParams(
            collective_id=0, has_side_effects=True, vmem_limit_bytes=57 * 1024 * 1024
        ),
    )(pair_list.T, slc_stack)


def solution(mesh):
    in_specs = (P("tm", None, "range", None), P("tm", None))
    out_specs = P("tm", None, "range", None)
    return jax.shard_map(local, mesh=mesh, in_specs=in_specs, out_specs=out_specs, check_vma=False)
```

time: 99.8 us -> 29.9 us (0.30); the launches traced: 98.5 us -> 29.7 us
  other arithmetic: 29.5 us -> 0 us
  local copies, waits for them, and re-layouts: 32.9 us -> 3.76 us
  Pallas kernels: 0 us -> 26 us
  matrix products: 14.9 us -> 0 us
  waiting for transfers between devices: 13.4 us -> 0 us
  starting transfers between devices: 7.5 us -> 0 us
    pallas_call x0 -> x1, Pallas kernels: none -> 26 us  [local(): pl.pallas_call(functools.partial(kernel, lax.axis_size('tm'), lax.axis_si...]
    add x5 -> x0, other arithmetic: 18.1 us -> none  [the longest x2 12.3 us: box_both(): summed = summed + padded[:, :, j:j + line_count]]
    gather x4 -> x0, local copies, waits for them, and re-layouts: 17 us -> none  [the longest x1 4.9 us: local(): ref_data = jnp.take(stack_all, ref_index, axis=0).astype(jnp.float32)]
    dot_general x4 -> x0, matrix products: 14.9 us -> none  [the longest x2 7.83 us: box_both(): jnp.einsum('kbil,io->kbol', head_block, band_near, precision=lax.Precisio...]
    slice x5 -> x0, local copies, waits for them, and re-layouts: 14.1 us -> none  [the longest x2 9.71 us: box_both(): padded[:, 128:col_count + 128].reshape((-1, block_count, 128, line_count))]
    ppermute x3 -> x0, waiting for transfers between devices: 13.4 us -> none  [passed_along(): return lax.ppermute(shard, axis, pairs)]
    ppermute x3 -> x0, starting transfers between devices: 7.5 us -> none  [passed_along(): return lax.ppermute(shard, axis, pairs)]
    convert_element_type x2 -> x0, other arithmetic: 5.05 us -> none  [the longest x1 2.81 us: local(): sec_data = jnp.take(stack_all, sec_index, axis=0).astype(jnp.float32)]
  transfers between devices with their start and end apart: 3 -> 0, of which waited for: 1 -> 0; matrix products, arithmetic and copies ran while one was open for 2% -> 0% of each run, Pallas kernels for 0% -> 0%
where the time goes in v1:
time: 29.9 us; the launch traced here: 29.7 us
  Pallas kernels  26 us (87%)
  local copies, waits for them, and re-layouts  3.76 us (13%)
    pallas_call x1, Pallas kernels, local(): pl.pallas_call(functools.partial(kernel, lax.axis_size('tm'), lax.axis_si...  26 us
    unnamed x1, local copies, waits for them, and re-layouts  3.76 us

profile of v1, /device:TPU:17, one launch (start us, length us, event | category | flops | bytes accessed | tf_op | source)
XLA Modules:
  0.0 29.7 jit_solution(16535012017543928128)
XLA Ops:
  0.0 26.0 %shard_map.28 = bf16[6,2,1024,128]{3,2,1,0:T(8,128)(2,1)} custom-call(s32[2,6]{1,0:T(2,128)} %bitcast.1, bf16[4,2,1024,128]{3,2,1,0:T(8,128)(2,1)} %slc_ref.1), custom_call_target="tpu_custom_call" | custom-call | tf_op jit(solution)/shard_map/pallas_call | solution.py:209
  26.0 3.8 %copy.4 = bf16[6,2,1024,128]{3,2,1,0:T(8,128)(2,1)} copy(bf16[6,2,1024,128]{3,2,1,0:T(8,128)(2,1)} %shard_map.28) | data formatting | bytes 6291456

commit v2 on v1

--- a/solution.py
+++ b/solution.py
@@ -12,6 +12,7 @@
 LOOK_RG = 20
 RIM = 32
 CHUNK = 128
+GROUP = 1
 EPSILON = 1e-06
 MESH = pl.DeviceIdType.MESH
 
@@ -144,18 +145,25 @@
     band = jnp.where(near, 1.0, 0.0).astype(jnp.bfloat16)
     first_acq = tm * acq_dev
 
-    def box(k, value):
-        field[k] = value
-        twos[k] = field[k, 0 : CHUNK + 24, :] + field[k, 1 : CHUNK + 25, :]
-        fours[k] = twos[k, 0 : CHUNK + 16, :] + twos[k, 2 : CHUNK + 18, :]
-        running = fours[k, 0:CHUNK, :]
-        for j in range(4, LOOK_RG, 4):
-            running = running + fours[k, j : j + CHUNK, :]
-        high = running.astype(jnp.bfloat16)
-        low = (running - high.astype(jnp.float32)).astype(jnp.bfloat16)
-        return jnp.dot(
-            jnp.concatenate([high, low], axis=1), band, preferred_element_type=jnp.float32
+    def box(slot, values):
+        parts = []
+        for k, value in enumerate(values, slot):
+            field[k] = value
+        for k in range(slot, slot + len(values)):
+            twos[k] = field[k, 0 : CHUNK + 24, :] + field[k, 1 : CHUNK + 25, :]
+        for k in range(slot, slot + len(values)):
+            fours[k] = twos[k, 0 : CHUNK + 16, :] + twos[k, 2 : CHUNK + 18, :]
+        for k in range(slot, slot + len(values)):
+            running = fours[k, 0:CHUNK, :]
+            for j in range(4, LOOK_RG, 4):
+                running = running + fours[k, j : j + CHUNK, :]
+            high = running.astype(jnp.bfloat16)
+            low = (running - high.astype(jnp.float32)).astype(jnp.bfloat16)
+            parts.append(jnp.concatenate([high, low], axis=1))
+        summed = jnp.dot(
+            jnp.concatenate(parts, axis=0), band, preferred_element_type=jnp.float32
         )
+        return [summed[k * CHUNK : (k + 1) * CHUNK] for k in range(len(values))]
 
     @pl.loop(0, n_chunks)
     def _(i):
@@ -169,21 +177,32 @@
         start = pl.multiple_of(c * CHUNK, CHUNK)
         at = pl.ds(start, CHUNK)
         ext = pl.ds(start, CHUNK + RIM)
+        powers = []
         for k in range(n_acq):
             source = own.at[k] if k < acq_dev else recv.at[k - acq_dev]
             real = source[0, ext, :].astype(jnp.float32)
             imag = source[1, ext, :].astype(jnp.float32)
             work[k, 0] = real
             work[k, 1] = imag
-            boxed[k] = box(k % 2, real * real + imag * imag)
-        for p in range(n_pairs):
-            ref = jnp.clip(pair_ref[0, p] - first_acq, 0, n_acq - 1)
-            sec = jnp.clip(pair_ref[1, p] - first_acq, 0, n_acq - 1)
-            r0, r1 = work[ref, 0], work[ref, 1]
-            s0, s1 = work[sec, 0], work[sec, 1]
-            norm = lax.rsqrt(boxed[ref] * boxed[sec] + EPSILON)
-            out_ref[p, 0, at, :] = (box(0, r0 * s0 + r1 * s1) * norm).astype(out_ref.dtype)
-            out_ref[p, 1, at, :] = (box(1, r1 * s0 - r0 * s1) * norm).astype(out_ref.dtype)
+            powers.append(real * real + imag * imag)
+        for k, value in enumerate(box(0, powers)):
+            boxed[k] = value
+        slot = n_acq
+        for first in range(0, n_pairs, GROUP):
+            group = range(first, min(first + GROUP, n_pairs))
+            products, norms = [], []
+            for p in group:
+                ref = jnp.clip(pair_ref[0, p] - first_acq, 0, n_acq - 1)
+                sec = jnp.clip(pair_ref[1, p] - first_acq, 0, n_acq - 1)
+                r0, r1 = work[ref, 0], work[ref, 1]
+                s0, s1 = work[sec, 0], work[sec, 1]
+                products += [r0 * s0 + r1 * s1, r1 * s0 - r0 * s1]
+                norms.append(lax.rsqrt(boxed[ref] * boxed[sec] + EPSILON))
+            summed = box(slot, products)
+            slot += len(products)
+            for q, p in enumerate(group):
+                out_ref[p, 0, at, :] = (summed[2 * q] * norms[q]).astype(out_ref.dtype)
+                out_ref[p, 1, at, :] = (summed[2 * q + 1] * norms[q]).astype(out_ref.dtype)
 
     @pl.when(has_left)
     def _():
@@ -205,6 +224,7 @@
     n_pairs = pair_list.shape[0]
     n_acq = acq_dev + LAG_MAX
     n_chunks = cols // CHUNK
+    n_fields = n_acq + 2 * n_pairs
     f32 = jnp.float32
     return pl.pallas_call(
         functools.partial(kernel, lax.axis_size("tm"), lax.axis_size("range")),
@@ -218,9 +238,9 @@
             pltpu.VMEM((acq_dev, 2, cols + RIM, lines), jnp.bfloat16),
             pltpu.VMEM((LAG_MAX, 2, cols + RIM, lines), jnp.bfloat16),
             pltpu.VMEM((n_acq, 2, CHUNK + RIM, lines), f32),
-            pltpu.VMEM((2, CHUNK + RIM, lines), f32),
-            pltpu.VMEM((2, CHUNK + 24, lines), f32),
-            pltpu.VMEM((2, CHUNK + 16, lines), f32),
+            pltpu.VMEM((n_fields, CHUNK + RIM, lines), f32),
+            pltpu.VMEM((n_fields, CHUNK + 24, lines), f32),
+            pltpu.VMEM((n_fields, CHUNK + 16, lines), f32),
             pltpu.VMEM((n_acq, CHUNK, lines), f32),
             pltpu.SemaphoreType.DMA((n_chunks,)),
             pltpu.SemaphoreType.DMA((n_chunks,)),
@@ -229,9 +249,12 @@
             pltpu.SemaphoreType.DMA((2,)),
         ],
         compiler_params=pltpu.CompilerParams(
-            collective_id=0, has_side_effects=True, vmem_limit_bytes=57 * 1024 * 1024
+            collective_id=0, has_side_effects=True, vmem_limit_bytes=32 * 1024 * 1024
         ),
-    )(pair_list.T, slc_stack)
+    )(
+        pltpu.with_memory_space_constraint(pair_list.T, pltpu.HBM),
+        pltpu.with_memory_space_constraint(slc_stack, pltpu.HBM),
+    )
 
 
 def solution(mesh):

time: 29.9 us -> 26 us (0.87)
  local copies, waits for them, and re-layouts: 3.76 us -> 1.67 us
  Pallas kernels: 26 us -> 24.1 us
    unnamed x1, local copies, waits for them, and re-layouts: 3.76 us -> 1.67 us
    pallas_call x1, Pallas kernels: 26 us -> 24.1 us  [local(): pl.pallas_call(functools.partial(kernel, lax.axis_size('tm'), lax.axis_si...]
where the time goes in v2:
time: 26 us; the launch traced here: 25.8 us
  Pallas kernels  24.1 us (93%)
  local copies, waits for them, and re-layouts  1.67 us (6%)
    pallas_call x1, Pallas kernels, local(): pl.pallas_call(functools.partial(kernel, lax.axis_size('tm'), lax.axis_si...  24.1 us
    unnamed x1, local copies, waits for them, and re-layouts  1.67 us

profile of v2, /device:TPU:17, one launch (start us, length us, event | category | flops | bytes accessed | tf_op | source)
XLA Modules:
  0.0 25.8 jit_solution(11566232963720751739)
XLA Ops:
  0.0 24.1 %shard_map.28 = bf16[6,2,1024,128]{3,2,1,0:T(8,128)(2,1)S(1)} custom-call(s32[2,6]{1,0:T(2,128)} %bitcast.1, bf16[4,2,1024,128]{3,2,1,0:T(8,128)(2,1)} %slc_ref.1), custom_call_target="tpu_custom_call" | custom-call | tf_op jit(solution)/shard_map/pallas_call | solution.py:229
  24.1 1.7 %copy.4 = bf16[6,2,1024,128]{3,2,1,0:T(8,128)(2,1)} copy(bf16[6,2,1024,128]{3,2,1,0:T(8,128)(2,1)S(1)} %shard_map.28) | data formatting | bytes 6291456

commit v3 on v1

v3 whole, which is shorter than its diff:
```python
import functools

import jax
import jax.numpy as jnp
from jax import lax
from jax.experimental import pallas as pl
from jax.experimental.pallas import tpu as pltpu
from jax.sharding import PartitionSpec as P

LAG_MAX = 3
LOOK_AZ = 5
LOOK_RG = 20
RIM = 32
CHUNK = 128
EPSILON = 1e-06
MESH = pl.DeviceIdType.MESH


def band_matrix(lines):
    half = LOOK_AZ // 2
    from_line = lax.rem(lax.broadcasted_iota(jnp.int32, (2 * lines, lines), 0), lines)
    to_line = lax.broadcasted_iota(jnp.int32, (2 * lines, lines), 1)
    near = (from_line - to_line >= -half) & (from_line - to_line <= LOOK_AZ - 1 - half)
    return jnp.where(near, 1.0, 0.0).astype(jnp.bfloat16)


def box(slot, values, band, field, twos, fours):
    parts = []
    slots = range(slot, slot + len(values))
    for k, value in zip(slots, values):
        field[k] = value
    for k in slots:
        twos[k] = field[k, 0 : CHUNK + 24, :] + field[k, 1 : CHUNK + 25, :]
    for k in slots:
        fours[k] = twos[k, 0 : CHUNK + 16, :] + twos[k, 2 : CHUNK + 18, :]
    for k in slots:
        running = fours[k, 0:CHUNK, :]
        for j in range(4, LOOK_RG, 4):
            running = running + fours[k, j : j + CHUNK, :]
        high = running.astype(jnp.bfloat16)
        low = (running - high.astype(jnp.float32)).astype(jnp.bfloat16)
        parts.append(jnp.concatenate([high, low], axis=1))
    summed = jnp.dot(jnp.concatenate(parts, axis=0), band, preferred_element_type=jnp.float32)
    return [summed[k * CHUNK : (k + 1) * CHUNK] for k in range(len(values))]


def coherence(pair_ref, first_acq, work, boxed, band, field, twos, fours, emit):
    n_acq = work.shape[0]
    n_pairs = pair_ref.shape[1]
    powers = [work[k, 0] * work[k, 0] + work[k, 1] * work[k, 1] for k in range(n_acq)]
    for k, value in enumerate(box(0, powers, band, field, twos, fours)):
        boxed[k] = value
    slot = n_acq
    for p in range(n_pairs):
        ref = jnp.clip(pair_ref[0, p] - first_acq, 0, n_acq - 1)
        sec = jnp.clip(pair_ref[1, p] - first_acq, 0, n_acq - 1)
        r0, r1 = work[ref, 0], work[ref, 1]
        s0, s1 = work[sec, 0], work[sec, 1]
        norm = lax.rsqrt(boxed[ref] * boxed[sec] + EPSILON)
        products = [r0 * s0 + r1 * s1, r1 * s0 - r0 * s1]
        real, imag = box(slot, products, band, field, twos, fours)
        slot += 2
        emit(p, (real * norm).astype(jnp.bfloat16), (imag * norm).astype(jnp.bfloat16))


def kernel(
    n_tm,
    n_range,
    pair_ref,
    slc_ref,
    out_ref,
    last_ref,
    own,
    recv,
    work,
    field,
    twos,
    fours,
    boxed,
    own_sem,
    send_sem,
    recv_sem,
    rim_send,
    rim_recv,
):
    tm = lax.axis_index("tm")
    rg = lax.axis_index("range")
    acq_dev, _, cols, lines = slc_ref.shape
    n_chunks = cols // CHUNK
    n_acq = acq_dev + LAG_MAX
    has_next = tm < n_tm - 1
    has_prev = tm > 0
    has_right = rg < n_range - 1
    has_left = rg > 0

    own_copy = pltpu.make_async_copy(slc_ref, own.at[:, :, pl.ds(0, cols), :], own_sem)

    def piece_copy(k, at):
        return pltpu.make_async_remote_copy(
            src_ref=slc_ref.at[pl.ds(0, LAG_MAX), :, at, :],
            dst_ref=recv.at[:, :, at, :],
            send_sem=send_sem.at[k],
            recv_sem=recv_sem.at[k],
            device_id=(tm - 1, rg),
            device_id_type=MESH,
        )

    def middle_piece(k):
        return piece_copy(k, pl.ds(pl.multiple_of(k * CHUNK + RIM, RIM), CHUNK))

    first_piece = piece_copy(0, pl.ds(0, CHUNK + RIM))
    last_piece = piece_copy(n_chunks - 1, pl.ds(cols - CHUNK + RIM, CHUNK - RIM))
    rim_copy = pltpu.make_async_remote_copy(
        src_ref=slc_ref.at[:, :, pl.ds(0, RIM), :],
        dst_ref=own.at[:, :, pl.ds(cols, RIM), :],
        send_sem=rim_send.at[0],
        recv_sem=rim_recv.at[0],
        device_id=(tm, rg - 1),
        device_id_type=MESH,
    )
    corner_copy = pltpu.make_async_remote_copy(
        src_ref=recv.at[:, :, pl.ds(0, RIM), :],
        dst_ref=recv.at[:, :, pl.ds(cols, RIM), :],
        send_sem=rim_send.at[1],
        recv_sem=rim_recv.at[1],
        device_id=(tm, rg - 1),
        device_id_type=MESH,
    )

    barrier = pltpu.get_barrier_semaphore()

    @pl.when(has_next)
    def _():
        pl.semaphore_signal(barrier, inc=1, device_id=(tm + 1, rg), device_id_type=MESH)

    @pl.when(has_right)
    def _():
        pl.semaphore_signal(barrier, inc=1, device_id=(tm, rg + 1), device_id_type=MESH)

    own_copy.start()

    @pl.when(has_prev | has_left)
    def _():
        pl.semaphore_wait(barrier, jnp.where(has_prev, 1, 0) + jnp.where(has_left, 1, 0))

    @pl.when(has_prev)
    def _():
        first_piece.start()

    @pl.when(has_left)
    def _():
        rim_copy.start()

    @pl.when(has_prev)
    def _():
        @pl.loop(1, n_chunks - 1)
        def _(k):
            middle_piece(k).start()

        last_piece.start()

    @pl.when(jnp.logical_not(has_next))
    def _():
        recv[...] = jnp.zeros_like(recv)

    @pl.when(has_next & jnp.logical_not(has_right))
    def _():
        recv[:, :, cols:, :] = jnp.zeros((LAG_MAX, 2, RIM, lines), recv.dtype)

    @pl.when(jnp.logical_not(has_right))
    def _():
        own[:, :, cols:, :] = jnp.zeros((acq_dev, 2, RIM, lines), own.dtype)

    band = band_matrix(lines)
    own_copy.wait()

    def gather(target, start):
        ext = pl.ds(start, CHUNK + RIM)
        for k in range(n_acq):
            source = own.at[k] if k < acq_dev else recv.at[k - acq_dev]
            target[k, 0] = source[0, ext, :].astype(jnp.float32)
            target[k, 1] = source[1, ext, :].astype(jnp.float32)

    @pl.when(has_next)
    def _():
        first_piece.wait_recv()

    @pl.when(has_next & has_left)
    def _():
        corner_copy.start()

    @pl.loop(0, n_chunks - 1)
    def _(c):
        @pl.when(has_next & (c > 0))
        def _():
            middle_piece(c).wait_recv()

        start = pl.multiple_of(c * CHUNK, CHUNK)
        gather(work, start)

        def emit(p, real, imag):
            out_ref[p, 0, pl.ds(start, CHUNK), :] = real
            out_ref[p, 1, pl.ds(start, CHUNK), :] = imag

        coherence(pair_ref, tm * acq_dev, work, boxed, band, field, twos, fours, emit)

    @pl.when(has_right)
    def _():
        rim_copy.wait_recv()

    @pl.when(has_next & has_right)
    def _():
        corner_copy.wait_recv()

    @pl.when(has_next)
    def _():
        last_piece.wait_recv()

    gather(last_ref, cols - CHUNK)

    @pl.when(has_left)
    def _():
        rim_copy.wait_send()

    @pl.when(has_next & has_left)
    def _():
        corner_copy.wait_send()

    @pl.when(has_prev)
    def _():
        first_piece.wait_send()

        @pl.loop(1, n_chunks - 1)
        def _(k):
            middle_piece(k).wait_send()

        last_piece.wait_send()


def finish(pair_ref, done_ref, work, out_ref, last, field, twos, fours, boxed, done_sem, last_sem):
    n_pairs, _, cols, lines = out_ref.shape
    n_acq = work.shape[0]
    before = pl.ds(0, cols - CHUNK)
    after = pl.ds(cols - CHUNK, CHUNK)
    early = [
        pltpu.make_async_copy(done_ref.at[p, :, before], out_ref.at[p, :, before], done_sem.at[p])
        for p in range(n_pairs)
    ]
    late = [
        pltpu.make_async_copy(last.at[p], out_ref.at[p, :, after], last_sem.at[p])
        for p in range(n_pairs)
    ]
    for copy in early:
        copy.start()

    def emit(p, real, imag):
        last[p, 0] = real
        last[p, 1] = imag
        late[p].start()

    first_acq = lax.axis_index("tm") * (n_acq - LAG_MAX)
    coherence(
        pair_ref, first_acq, work, boxed, band_matrix(lines), field, twos, fours, emit
    )
    for copy in early + late:
        copy.wait()


def local(slc_stack, pair_list):
    acq_dev, _, cols, lines = slc_stack.shape
    n_pairs = pair_list.shape[0]
    n_acq = acq_dev + LAG_MAX
    n_chunks = cols // CHUNK
    n_fields = n_acq + 2 * n_pairs
    f32, bf16 = jnp.float32, jnp.bfloat16
    box_scratch = [
        pltpu.VMEM((n_fields, CHUNK + RIM, lines), f32),
        pltpu.VMEM((n_fields, CHUNK + 24, lines), f32),
        pltpu.VMEM((n_fields, CHUNK + 16, lines), f32),
        pltpu.VMEM((n_acq, CHUNK, lines), f32),
    ]
    smem = pl.BlockSpec(memory_space=pltpu.SMEM)
    vmem = pl.BlockSpec(memory_space=pltpu.VMEM)
    hbm = pl.BlockSpec(memory_space=pltpu.HBM)
    pairs = pltpu.with_memory_space_constraint(pair_list.T, pltpu.HBM)
    done, last = pl.pallas_call(
        functools.partial(kernel, lax.axis_size("tm"), lax.axis_size("range")),
        out_shape=(
            pltpu.VMEM((n_pairs, 2, cols, lines), bf16),
            pltpu.VMEM((n_acq, 2, CHUNK + RIM, lines), f32),
        ),
        in_specs=[smem, hbm],
        out_specs=(vmem, vmem),
        scratch_shapes=[
            pltpu.VMEM((acq_dev, 2, cols + RIM, lines), bf16),
            pltpu.VMEM((LAG_MAX, 2, cols + RIM, lines), bf16),
            pltpu.VMEM((n_acq, 2, CHUNK + RIM, lines), f32),
            *box_scratch,
            pltpu.SemaphoreType.DMA,
            pltpu.SemaphoreType.DMA((n_chunks,)),
            pltpu.SemaphoreType.DMA((n_chunks,)),
            pltpu.SemaphoreType.DMA((2,)),
            pltpu.SemaphoreType.DMA((2,)),
        ],
        compiler_params=pltpu.CompilerParams(
            collective_id=0, has_side_effects=True, vmem_limit_bytes=32 * 1024 * 1024
        ),
    )(pairs, pltpu.with_memory_space_constraint(slc_stack, pltpu.HBM))
    return pl.pallas_call(
        finish,
        out_shape=jax.ShapeDtypeStruct((n_pairs, 2, cols, lines), bf16),
        in_specs=[smem, vmem, vmem],
        out_specs=hbm,
        scratch_shapes=[
            pltpu.VMEM((n_pairs, 2, CHUNK, lines), bf16),
            *box_scratch,
            pltpu.SemaphoreType.DMA((n_pairs,)),
            pltpu.SemaphoreType.DMA((n_pairs,)),
        ],
        compiler_params=pltpu.CompilerParams(vmem_limit_bytes=32 * 1024 * 1024),
    )(pair_list.T, done, last)


def solution(mesh):
    in_specs = (P("tm", None, "range", None), P("tm", None))
    out_specs = P("tm", None, "range", None)
    return jax.shard_map(local, mesh=mesh, in_specs=in_specs, out_specs=out_specs, check_vma=False)
```

time: 29.9 us -> 26.7 us (0.89)
  local copies, waits for them, and re-layouts: 3.76 us -> 0.67 us
    pallas_call x1, Pallas kernels: 26 us -> 22.5 us  [local(): pl.pallas_call(functools.partial(kernel, lax.axis_size('tm'), lax.axis_si...]
    pallas_call x0 -> x1, Pallas kernels: none -> 3.32 us  [local(): pl.pallas_call(finish, out_shape=jax.ShapeDtypeStruct((n_pairs, 2, cols,...]
    unnamed x1 -> x2, local copies, waits for them, and re-layouts: 3.76 us -> 0.67 us
where the time goes in v3:
time: 26.7 us; the launch traced here: 26.5 us
  Pallas kernels  25.8 us (97%)
  local copies, waits for them, and re-layouts  0.67 us (3%)
    pallas_call x1, Pallas kernels, local(): pl.pallas_call(functools.partial(kernel, lax.axis_size('tm'), lax.axis_si...  22.5 us
    pallas_call x1, Pallas kernels, local(): pl.pallas_call(finish, out_shape=jax.ShapeDtypeStruct((n_pairs, 2, cols,...  3.32 us
    unnamed x2, local copies, waits for them, and re-layouts  0.67 us

profile of v3, /device:TPU:17, one launch (start us, length us, event | category | flops | bytes accessed | tf_op | source)
XLA Modules:
  0.0 26.5 jit_solution(15944760124227902267)
XLA Ops:
  0.0 22.5 %shard_map.28 = (bf16[6,2,1024,128]{3,2,1,0:T(8,128)(2,1)S(1)}, f32[7,2,160,128]{3,2,1,0:T(8,128)S(1)}) custom-call(s32[2,6]{1,0:T(2,128)} %bitcast.1, bf16[4,2,1024,128]{3,2,1,0:T(8,128)(2,1)} %slc_ref.1), custom_call_target="tpu_custom_call" | custom-call | tf_op jit(solution)/shard_map/pallas_call | solution.py:286
  22.5 0.0 copy-start
  22.5 0.7 %copy-done = s32[6,2]{0,1:T(2,128)S(1)} copy-done((s32[6,2]{0,1:T(2,128)S(1)}, s32[6,2]{0,1:T(2,128)}, u32[]{:S(2)}) %copy-start) | copy-done | bytes 72
  23.2 3.3 %shard_map.29 = bf16[6,2,1024,128]{3,2,1,0:T(8,128)(2,1)} custom-call(s32[2,6]{1,0:T(2,128)S(1)} %bitcast.2, bf16[6,2,1024,128]{3,2,1,0:T(8,128)(2,1)S(1)} %get-tuple-element.7.done_ref, f32[7,2,160,128]{3,2,1,0:T(8,128)S(1)} %get-tuple-element.8.work), custom_call_target="tpu_custom_call" | custom-call | tf_op jit(solution)/shard_map/pallas_call | solution.py:309
Async XLA Ops:
  22.5 0.7 %copy-start = (s32[6,2]{0,1:T(2,128)S(1)}, s32[6,2]{0,1:T(2,128)}, u32[]{:S(2)}) copy-start(s32[6,2]{0,1:T(2,128)} %param.3) | copy-start | bytes 148

commit v4 on v3

--- a/solution.py
+++ b/solution.py
@@ -69,7 +69,6 @@
     pair_ref,
     slc_ref,
     out_ref,
-    last_ref,
     own,
     recv,
     work,
@@ -181,6 +180,15 @@
             target[k, 0] = source[0, ext, :].astype(jnp.float32)
             target[k, 1] = source[1, ext, :].astype(jnp.float32)
 
+    def chunk(start):
+        gather(work, start)
+
+        def emit(p, real, imag):
+            out_ref[p, 0, pl.ds(start, CHUNK), :] = real
+            out_ref[p, 1, pl.ds(start, CHUNK), :] = imag
+
+        coherence(pair_ref, tm * acq_dev, work, boxed, band, field, twos, fours, emit)
+
     @pl.when(has_next)
     def _():
         first_piece.wait_recv()
@@ -195,14 +203,7 @@
         def _():
             middle_piece(c).wait_recv()
 
-        start = pl.multiple_of(c * CHUNK, CHUNK)
-        gather(work, start)
-
-        def emit(p, real, imag):
-            out_ref[p, 0, pl.ds(start, CHUNK), :] = real
-            out_ref[p, 1, pl.ds(start, CHUNK), :] = imag
-
-        coherence(pair_ref, tm * acq_dev, work, boxed, band, field, twos, fours, emit)
+        chunk(pl.multiple_of(c * CHUNK, CHUNK))
 
     @pl.when(has_right)
     def _():
@@ -216,7 +217,7 @@
     def _():
         last_piece.wait_recv()
 
-    gather(last_ref, cols - CHUNK)
+    chunk(cols - CHUNK)
 
     @pl.when(has_left)
     def _():
@@ -235,35 +236,6 @@
             middle_piece(k).wait_send()
 
         last_piece.wait_send()
-
-
-def finish(pair_ref, done_ref, work, out_ref, last, field, twos, fours, boxed, done_sem, last_sem):
-    n_pairs, _, cols, lines = out_ref.shape
-    n_acq = work.shape[0]
-    before = pl.ds(0, cols - CHUNK)
-    after = pl.ds(cols - CHUNK, CHUNK)
-    early = [
-        pltpu.make_async_copy(done_ref.at[p, :, before], out_ref.at[p, :, before], done_sem.at[p])
-        for p in range(n_pairs)
-    ]
-    late = [
-        pltpu.make_async_copy(last.at[p], out_ref.at[p, :, after], last_sem.at[p])
-        for p in range(n_pairs)
-    ]
-    for copy in early:
-        copy.start()
-
-    def emit(p, real, imag):
-        last[p, 0] = real
-        last[p, 1] = imag
-        late[p].start()
-
-    first_acq = lax.axis_index("tm") * (n_acq - LAG_MAX)
-    coherence(
-        pair_ref, first_acq, work, boxed, band_matrix(lines), field, twos, fours, emit
-    )
-    for copy in early + late:
-        copy.wait()
 
 
 def local(slc_stack, pair_list):
@@ -283,14 +255,11 @@
     vmem = pl.BlockSpec(memory_space=pltpu.VMEM)
     hbm = pl.BlockSpec(memory_space=pltpu.HBM)
     pairs = pltpu.with_memory_space_constraint(pair_list.T, pltpu.HBM)
-    done, last = pl.pallas_call(
+    return pl.pallas_call(
         functools.partial(kernel, lax.axis_size("tm"), lax.axis_size("range")),
-        out_shape=(
-            pltpu.VMEM((n_pairs, 2, cols, lines), bf16),
-            pltpu.VMEM((n_acq, 2, CHUNK + RIM, lines), f32),
-        ),
+        out_shape=pltpu.VMEM((n_pairs, 2, cols, lines), bf16),
         in_specs=[smem, hbm],
-        out_specs=(vmem, vmem),
+        out_specs=vmem,
         scratch_shapes=[
             pltpu.VMEM((acq_dev, 2, cols + RIM, lines), bf16),
             pltpu.VMEM((LAG_MAX, 2, cols + RIM, lines), bf16),
@@ -306,19 +275,6 @@
             collective_id=0, has_side_effects=True, vmem_limit_bytes=32 * 1024 * 1024
         ),
     )(pairs, pltpu.with_memory_space_constraint(slc_stack, pltpu.HBM))
-    return pl.pallas_call(
-        finish,
-        out_shape=jax.ShapeDtypeStruct((n_pairs, 2, cols, lines), bf16),
-        in_specs=[smem, vmem, vmem],
-        out_specs=hbm,
-        scratch_shapes=[
-            pltpu.VMEM((n_pairs, 2, CHUNK, lines), bf16),
-            *box_scratch,
-            pltpu.SemaphoreType.DMA((n_pairs,)),
-            pltpu.SemaphoreType.DMA((n_pairs,)),
-        ],
-        compiler_params=pltpu.CompilerParams(vmem_limit_bytes=32 * 1024 * 1024),
-    )(pair_list.T, done, last)
 
 
 def solution(mesh):

time: 26.7 us -> 25.4 us (0.951)
  Pallas kernels: 25.8 us -> 23.5 us
  local copies, waits for them, and re-layouts: 0.67 us -> 1.67 us
    pallas_call x1 -> x0, Pallas kernels: 3.32 us -> none  [local(): pl.pallas_call(finish, out_shape=jax.ShapeDtypeStruct((n_pairs, 2, cols,...]
    pallas_call x1, Pallas kernels: 22.5 us -> 23.5 us  [local(): pl.pallas_call(functools.partial(kernel, lax.axis_size('tm'), lax.axis_si...]
    unnamed x2 -> x1, local copies, waits for them, and re-layouts: 0.67 us -> 1.67 us
where the time goes in v4:
time: 25.4 us; the launch traced here: 25.2 us
  Pallas kernels  23.5 us (93%)
  local copies, waits for them, and re-layouts  1.67 us (7%)
    pallas_call x1, Pallas kernels, local(): pl.pallas_call(functools.partial(kernel, lax.axis_size('tm'), lax.axis_si...  23.5 us
    unnamed x1, local copies, waits for them, and re-layouts  1.67 us

profile of v4, /device:TPU:17, one launch (start us, length us, event | category | flops | bytes accessed | tf_op | source)
XLA Modules:
  0.0 25.2 jit_solution(14891950633024637683)
XLA Ops:
  0.0 23.5 %shard_map.28 = bf16[6,2,1024,128]{3,2,1,0:T(8,128)(2,1)S(1)} custom-call(s32[2,6]{1,0:T(2,128)} %bitcast.1, bf16[4,2,1024,128]{3,2,1,0:T(8,128)(2,1)} %slc_ref.1), custom_call_target="tpu_custom_call" | custom-call | tf_op jit(solution)/shard_map/pallas_call | solution.py:258
  23.5 1.7 %copy.4 = bf16[6,2,1024,128]{3,2,1,0:T(8,128)(2,1)} copy(bf16[6,2,1024,128]{3,2,1,0:T(8,128)(2,1)S(1)} %shard_map.28) | data formatting | bytes 6291456
